TPU v7x, 128 devices: a whole 4x4x4 slice. The times are simulated.
128 devices in a mesh: enc: 2 (over y_lo), fsdp: 64 (over x, y_hi, z, core).
Axes of the slice: x: 4, y: 4 (y_hi: 2, y_lo: 2; y = y_hi * 2 + y_lo), z: 4, core: 2. Of those that a mesh axis runs over, the one named last changes fastest.
Arguments:
- dino_feats: bfloat16 [128, 2, 256, 1024], P('fsdp', 'enc'), may hold values from -16 to 16
- siglip_feats: bfloat16 [128, 2, 256, 1152], P('fsdp', 'enc'), may hold values from -16 to 16
- proj_weight: bfloat16 [2176, 4352], P('fsdp', 'enc'), may hold values from -0.125 to 0.125
- proj_bias: float32 [4352], P('enc'), may hold values from -3 to 3
- hidden_grad: bfloat16 [128, 512, 4352], P('fsdp', None, 'enc'), may hold values from -6 to 6
Outputs:
- hidden: bfloat16 [128, 512, 4352], P('fsdp', None, 'enc')
- weight_grad: float32 [2176, 4352], P('fsdp', 'enc')
- bias_grad: float32 [4352], P('enc')
- dino_grad: bfloat16 [128, 2, 256, 1024], P('fsdp', 'enc')
- siglip_grad: bfloat16 [128, 2, 256, 1152], P('fsdp', 'enc')
All inputs are finite; a program needn't handle non-finite values.
Results may differ from a plain program's by a relative error of at most 0.0059.
Values may be sent and summed in bfloat16 or wider, within the bound.
A program may use at most 192 MiB of HBM per device.

v0:
```python
import jax
import jax.numpy as jnp
from jax import lax
from jax.sharding import Mesh
from jax.sharding import PartitionSpec as P

DINO = 1024
FEAT = 2176
FSDP = ("fsdp_0", "fsdp_1", "fsdp_2", "fsdp_3")


def sent_together(arrays, axis, dim, along):
    ends, at = ([], 0)
    for a in arrays[:-1]:
        at += a.shape[along]
        ends.append(at)
    both = jnp.concatenate(arrays, axis=along)
    return tuple(jnp.split(lax.all_gather(both, axis, axis=dim, tiled=True), ends, axis=along))


def split_up(array, dim, length):
    before, after = (array.shape[:dim], array.shape[dim + 1 :])
    return jnp.moveaxis(array.reshape(*before, length, -1, *after), dim, 0)


def sum_by_chip_2(array, chips, core, dim):
    sizes = (lax.axis_size(chips), lax.axis_size(core))
    pieces = split_up(array, dim, sizes[0] * sizes[1])
    inside = pieces.shape[1:]
    pieces = pieces.reshape(*sizes, *inside).swapaxes(0, 1).reshape(-1, *inside)
    pieces = lax.psum_scatter(pieces, core, scatter_dimension=0, tiled=True)
    return lax.psum_scatter(pieces, chips, scatter_dimension=0, tiled=True)[0]


def sent_to_all(array, axis):
    length = lax.axis_size(axis)
    return lax.all_to_all(
        jnp.broadcast_to(array[None], (length, *array.shape)), axis, 0, 0, tiled=True
    )


def taken_together(array, axis):
    return sent_to_all(array, axis).sum(axis=0)


def swapped(array, axis, bit):
    return lax.ppermute(array, axis, [(i, i ^ 1 << bit) for i in range(lax.axis_size(axis))])


def gelu_exact(values):
    return jax.nn.gelu(values, approximate=False)


def shards(dino_feats, siglip_feats, proj_weight, proj_bias, hidden_grad):
    dino_pair, siglip_pair = sent_together((dino_feats, siglip_feats), "enc", 1, 3)
    lead_shape = dino_pair.shape[:3]
    feats = jnp.concatenate([dino_pair, siglip_pair], -1).reshape(-1, FEAT)
    width = proj_weight.shape[1]
    whole_weight = lax.all_gather(proj_weight, FSDP, axis=0, tiled=True)
    preact = jnp.dot(feats, whole_weight, preferred_element_type=jnp.float32)
    preact = preact + proj_bias
    activated, pull = jax.vjp(gelu_exact, preact)
    hidden_out = activated.astype(jnp.bfloat16).reshape(hidden_grad.shape)
    (local_grad,) = pull(hidden_grad.reshape(-1, width).astype(jnp.float32))
    local_grad = local_grad.astype(jnp.bfloat16)
    weight_grad = sum_by_chip_2(
        lax.dot_general(
            feats, local_grad, (((0,), (0,)), ((), ())), preferred_element_type=jnp.float32
        ),
        ("fsdp_0", "fsdp_1", "fsdp_2"),
        "fsdp_3",
        0,
    )
    bias_grad = taken_together(jnp.sum(local_grad.astype(jnp.float32), 0), FSDP)
    feat_part = lax.dot_general(
        local_grad, whole_weight, (((1,), (1,)), ((), ())), preferred_element_type=jnp.float32
    )
    feat_part = feat_part.astype(jnp.bfloat16).reshape(lead_shape + (FEAT,))
    own_image = lax.axis_index("enc")
    kept_half = lax.dynamic_slice_in_dim(feat_part, own_image, 1, 1)
    sent_half = lax.dynamic_slice_in_dim(feat_part, 1 - own_image, 1, 1)
    other_half = swapped(sent_half, "enc", 0)
    feat_grad = (kept_half.astype(jnp.float32) + other_half.astype(jnp.float32)).astype(
        jnp.bfloat16
    )
    return (hidden_out, weight_grad, bias_grad, feat_grad[..., :DINO], feat_grad[..., DINO:])


def solution(mesh):
    finer = Mesh(
        mesh.devices.reshape(mesh.shape["enc"], 4, 2, 4, 2),
        ("enc", "fsdp_0", "fsdp_1", "fsdp_2", "fsdp_3"),
    )
    in_specs = (
        P(FSDP, "enc", None, None),
        P(FSDP, "enc", None, None),
        P(FSDP, "enc"),
        P("enc"),
        P(FSDP, None, "enc"),
    )
    out_specs = (
        P(FSDP, None, "enc"),
        P(FSDP, "enc"),
        P("enc"),
        P(FSDP, "enc", None, None),
        P(FSDP, "enc", None, None),
    )
    return jax.shard_map(
        shards, mesh=finer, in_specs=in_specs, out_specs=out_specs, check_vma=False
    )
```

profile of v0, /device:TPU:0, one launch (start us, length us, event | category | flops | bytes accessed | tf_op | source)
XLA Modules:
  0.0 689.9 jit_solution(7756643836204835596)
XLA Ops:
  7.2 0.0 all-gather.4.cloned.1.call-start
  7.2 3.1 pad_maximum_fusion
  10.3 0.0 all-gather.4.cloned.1.call-update
  10.3 0.0 all-gather.6.cloned.1.call-start
  10.4 0.7 all-gather.6.cloned.1.call-update
  11.1 0.0 reduce-scatter.3.cloned.1.call-start
  11.1 64.1 %all-gather.4.cloned.1.call-done = bf16[2,2,256,2176]{3,2,1,0:T(8,128)(2,1)} async-done(((bf16[2,1,256,2176]{3,2,1,0:T(8,128)(2,1)}), bf16[2,2,256,2176]{3,2,1,0:T(8,128)(2,1)}) %all-gather.4.cloned.1.call-update) | async-done | bytes 4456464 | tf_op jit(solution)/shard_map/all_gather | solution.py:18
  75.2 6.5 copy.17
  81.7 7.3 %dot_general.15 = bf16[32,2,34,1024]{3,2,1,0:T(8,128)(2,1)} reshape(bf16[2176,1024]{1,0:T(8,128)(2,1)} %bitcast.27) | data formatting | bytes 8912896 | tf_op jit(solution)/shard_map/dot_general | solution.py:67
  89.0 0.0 copy-start.1
  89.0 80.0 %all-gather.6.cloned.1.call-done = bf16[64,34,2176]{2,1,0:T(8,128)(2,1)} async-done(((bf16[1,34,2176]{2,1,0:T(8,128)(2,1)}), bf16[64,34,2176]{2,1,0:T(8,128)(2,1)}) %all-gather.6.cloned.1.call-update) | async-done | bytes 9469968 | tf_op jit(solution)/shard_map/all_gather | solution.py:59
  169.0 13.7 %reshape.39 = bf16[2176,2176]{1,0:T(8,128)(2,1)} reshape(bf16[64,34,2176]{2,1,0:T(8,128)(2,1)} %all-gather.6.cloned.1.call-done) | data formatting | bytes 18939904
  182.7 0.0 copy-done.1
  182.7 42.3 %convert_reduce_fusion = (f32[2176]{0:T(1024)S(1)}, bf16[1024,2176]{1,0:T(8,128)(2,1)}, f32[1024,2176]{1,0:T(8,128)}, f32[1024,2176]{1,0:T(8,128)}) fusion(bf16[2,512,2176]{2,1,0:T(8,128)(2,1)} %param.9, f32[2176]{0:T(1024)S(1)} %copy-done.1, bf16[1024,2176]{1,0:T(8,128)(2,1)} %bitcast.30, bf16[2176,2176]{1,0:T(8,128)(2,1)} %reshape.39), kind=kOutput, calls=%fused_computation.12 | convolution fusion | flops 9866573824 | bytes 40682496 | tf_op jit(solution)/shard_map/dot_general | solution.py:60
  225.0 15.9 %convolution_bitcast_fusion = f32[2,32,34,2176]{3,2,0,1:T(8,128)S(1)} fusion(bf16[32,2,34,1024]{3,2,1,0:T(8,128)(2,1)} %dot_general.15, bf16[1024,2176]{1,0:T(8,128)(2,1)} %get-tuple-element.6), kind=kOutput, calls=%fused_computation.1 | convolution fusion | flops 9697230848 | bytes 27852800 | tf_op jit(solution)/shard_map/dot_general | solution.py:67
  240.9 12.0 %copy.18 = f32[2,32,34,2176]{3,1,0,2:T(8,128)} copy(f32[2,32,34,2176]{3,2,0,1:T(8,128)S(1)} %convolution_bitcast_fusion) | data formatting | bytes 37879808 | tf_op jit(solution)/shard_map/transpose | solution.py:30
  252.9 0.0 reduce-scatter.3.cloned.1.call-update
  252.9 0.0 all-reduce.3.cloned.1.call-start
  253.0 28.9 %reduce-scatter.3.cloned.1.call-done = f32[32,34,2176]{2,0,1:T(8,128)} async-done(((f32[64,34,2176]{2,0,1:T(8,128)}), f32[32,34,2176]{2,0,1:T(8,128)}) %reduce-scatter.3.cloned.1.call-update) | async-done | bytes 9469968 | tf_op jit(solution)/shard_map/reduce_scatter | solution.py:31
  281.9 0.0 all-reduce.3.cloned.1.call-update
  281.9 0.0 copy-start.2
  281.9 14.9 %convolution_convert_fusion = bf16[1024,2176]{1,0:T(8,128)(2,1)S(1)} fusion(bf16[1024,2176]{1,0:T(8,128)(2,1)} %get-tuple-element.6, bf16[2176,2176]{1,0:T(8,128)(2,1)} %reshape.39), kind=kOutput, calls=%fused_computation.27 | convolution fusion | flops 9699459072 | bytes 18382848 | tf_op jit(solution)/shard_map/dot_general | solution.py:75
  296.8 0.0 copy-start
  296.8 2.2 copy-done
  299.0 0.2 constant_dynamic-slice_fusion.1
  299.2 1.7 collective-permute-start
  300.9 0.0 copy-done.2
  300.9 0.6 dynamic-slice
  301.5 1.1 broadcast_in_dim.2
  302.6 10.0 %all-to-all-start = ((f32[64,1,2176]{2,1,0:T(1,128)}), f32[64,1,2176]{2,1,0:T(1,128)S(1)}, u32[]{:S(2)}, u32[]{:S(2)}) async-start(f32[64,1,2176]{2,1,0:T(1,128)} %broadcast_in_dim.2), calls=%async_computation.1 | async-start | bytes 1114112 | tf_op jit(solution)/shard_map/all_to_all | solution.py:37
  312.6 9.3 %multiply_convert_fusion = bf16[1024,2176]{1,0:T(8,128)(2,1)} fusion(f32[1024,2176]{1,0:T(8,128)} %get-tuple-element.7, f32[1024,2176]{1,0:T(8,128)} %get-tuple-element.8, f32[2176]{0:T(1024)S(1)} %copy-done.1), kind=kLoop, calls=%fused_computation.13 | loop fusion | flops 8912896 | bytes 22290944 | tf_op jit(solution)/shard_map/convert_element_type | solution.py:63
  321.8 95.2 %all-to-all-done = f32[64,1,2176]{2,1,0:T(1,128)S(1)} async-done(((f32[64,1,2176]{2,1,0:T(1,128)}), f32[64,1,2176]{2,1,0:T(1,128)S(1)}, u32[]{:S(2)}, u32[]{:S(2)}) %all-to-all-start) | async-done | bytes 557088 | tf_op jit(solution)/shard_map/all_to_all | solution.py:37
  417.0 1.0 reduce_sum.19
  418.0 0.0 collective-permute-done
  418.0 2.9 add_convert_fusion
  420.9 1.1 slice.10
  422.0 1.1 slice.9
  423.1 257.0 %all-reduce.3.cloned.1.call-done = f32[32,34,2176]{2,0,1:T(8,128)} async-done(((f32[32,34,2176]{2,0,1:T(8,128)}), f32[32,34,2176]{2,0,1:T(8,128)}) %all-reduce.3.cloned.1.call-update) | async-done | bytes 9469968
  680.1 2.5 constant_dynamic-slice_fusion
  682.6 0.8 copy.26
Async XLA Ops:
  7.2 68.0 %all-gather.4.cloned.1.call-start = ((), (), s32[]{:S(2)}) async-start(), calls=%async_computation.2 | async-start | bytes 6684672 | tf_op jit(solution)/shard_map/all_gather | solution.py:18
  10.3 158.6 %all-gather.6.cloned.1.call-start = ((), (), s32[]{:S(2)}) async-start(), calls=%async_computation.4 | async-start | bytes 11315200 | tf_op jit(solution)/shard_map/all_gather | solution.py:59
  11.1 270.8 %reduce-scatter.3.cloned.1.call-start = ((), (), s32[]{:S(2)}) async-start(), calls=%async_computation.3 | async-start | bytes 28409856 | tf_op jit(solution)/shard_map/reduce_scatter | solution.py:31
  89.0 93.8 %copy-start.1 = (f32[2176]{0:T(1024)S(1)}, f32[2176]{0:T(1024)}, u32[]{:S(2)}) copy-start(f32[2176]{0:T(1024)} %param.8) | copy-start | bytes 26116
  252.9 427.2 %all-reduce.3.cloned.1.call-start = ((), (), s32[]{:S(2)}) async-start(), calls=%async_computation.5 | async-start | bytes 18939904
  281.9 19.0 %copy-start.2 = (u32[128]{0:T(128)S(1)}, u32[128]{0:T(128)}, u32[]{:S(2)}) copy-start(u32[128]{0:T(128)} %constant.83) | copy-start | bytes 1540
  296.8 2.2 copy-start
  299.2 118.9 %collective-permute-start = (bf16[2,1,256,2176]{3,2,1,0:T(8,128)(2,1)S(1)}, bf16[2,1,256,2176]{3,2,1,0:T(8,128)(2,1)}, u32[]{:S(2)}, u32[]{:S(2)}) collective-permute-start(bf16[2,1,256,2176]{3,2,1,0:T(8,128)(2,1)S(1)} %constant_dynamic-slice_fusion.1), channel_id=1, source_target_pairs={{0,64},{64,0},{1,65},{65,1},{2,66},{66,2},{3,67},{67,3},{4,68},{68... | collective-permute-start | bytes 6684680 | tf_op jit(solution)/shard_map/ppermute | solution.py:47
  302.6 114.5 %all-to-all-start = ((f32[64,1,2176]{2,1,0:T(1,128)}), f32[64,1,2176]{2,1,0:T(1,128)S(1)}, u32[]{:S(2)}, u32[]{:S(2)}) async-start(f32[64,1,2176]{2,1,0:T(1,128)} %broadcast_in_dim.2), calls=%async_computation.1 | async-start | bytes 1114112 | tf_op jit(solution)/shard_map/all_to_all | solution.py:37
Sparse Core Ops, SparseCore 0:
  10.5 64.6 all-gather.3
  78.4 90.4 all-gather.5
  253.1 28.7 reduce-scatter.2
  284.3 395.7 all-reduce.2
where the time goes:
time: 691 us; the launch traced here: 690 us
  waiting for transfers between devices  526 us (76%)
  matrix products  73.1 us (11%)
  local copies, waits for them, and re-layouts  49 us (7%)
  other arithmetic  16.2 us (2%)
  between operations  13.8 us (2%)
  starting transfers between devices  11.8 us (2%)
    unnamed x5, waiting for transfers between devices  258 us
    all_to_all x1, waiting for transfers between devices, sent_to_all(): lax.all_to_all(jnp.broadcast_to(array[None], (length, *array.shape)), axi...  95.2 us
    all_gather x1, waiting for transfers between devices, shards(): whole_weight = lax.all_gather(proj_weight, FSDP, axis=0, tiled=True)  80 us
    all_gather x1, waiting for transfers between devices, sent_together(): lax.all_gather(both, axis, axis=dim, tiled=True)  64.1 us
    dot_general x1, matrix products, shards(): preact = jnp.dot(feats, whole_weight, preferred_element_type=jnp.float32)  42.3 us
    reduce_scatter x1, waiting for transfers between devices, sum_by_chip_2(): pieces = lax.psum_scatter(pieces, core, scatter_dimension=0, tiled=True)  28.9 us
    unnamed x10, local copies, waits for them, and re-layouts  19.8 us
    dot_general x1, matrix products, shards(): lax.dot_general(feats, local_grad, (((0,), (0,)), ((), ())), preferred_el...  15.9 us
  transfers between devices with their start and end apart: 6, of which 5 were waited for; matrix products, arithmetic and copies ran while one was open for 7% of the time, Pallas kernels for 0%

commit v1 on v0

--- a/solution.py
+++ b/solution.py
@@ -56,7 +56,9 @@
     lead_shape = dino_pair.shape[:3]
     feats = jnp.concatenate([dino_pair, siglip_pair], -1).reshape(-1, FEAT)
     width = proj_weight.shape[1]
-    whole_weight = lax.all_gather(proj_weight, FSDP, axis=0, tiled=True)
+    whole_weight = jnp.concatenate(
+        lax.all_to_all(jnp.stack([proj_weight] * lax.axis_size(FSDP)), FSDP, 0, 0), axis=0
+    )
     preact = jnp.dot(feats, whole_weight, preferred_element_type=jnp.float32)
     preact = preact + proj_bias
     activated, pull = jax.vjp(gelu_exact, preact)

time: 691 us -> 752 us (1.088)
  waiting for transfers between devices: 526 us -> 571 us
  starting transfers between devices: 11.8 us -> 23.7 us
    all_gather x1, waiting for transfers between devices: 64.1 us -> 174 us  [sent_together(): lax.all_gather(both, axis, axis=dim, tiled=True)]
    all_gather x1 -> x0, waiting for transfers between devices: 80 us -> none  [shards(): whole_weight = lax.all_gather(proj_weight, FSDP, axis=0, tiled=True)]
    reduce_scatter x1, waiting for transfers between devices: 28.9 us -> 43.9 us  [sum_by_chip_2(): pieces = lax.psum_scatter(pieces, core, scatter_dimension=0, tiled=True)]
    unnamed x10 -> x13, local copies, waits for them, and re-layouts: 19.8 us -> 6.02 us
    reshape x0 -> x1, local copies, waits for them, and re-layouts: none -> 13.7 us  [shards(): jnp.concatenate(lax.all_to_all(jnp.stack([proj_weight] * lax.axis_size(FS...]
    all_to_all x0 -> x1, starting transfers between devices: none -> 11.9 us  [shards(): lax.all_to_all(jnp.stack([proj_weight] * lax.axis_size(FSDP)), FSDP, 0, 0)]
    unnamed x5 -> x4, waiting for transfers between devices: 258 us -> 258 us
  transfers between devices with their start and end apart: 6 -> 6, of which waited for: 5 -> 4; matrix products, arithmetic and copies ran while one was open for 7% -> 6% of each run, Pallas kernels for 0% -> 0%
where the time goes in v1:
time: 752 us; the launch traced here: 751 us
  waiting for transfers between devices  571 us (76%)
  matrix products  73.1 us (10%)
  local copies, waits for them, and re-layouts  54.7 us (7%)
  starting transfers between devices  23.7 us (3%)
  other arithmetic  14.6 us (2%)
  between operations  13.8 us (2%)
    unnamed x4, waiting for transfers between devices  258 us
    all_gather x1, waiting for transfers between devices, sent_together(): lax.all_gather(both, axis, axis=dim, tiled=True)  174 us
    all_to_all x1, waiting for transfers between devices, sent_to_all(): lax.all_to_all(jnp.broadcast_to(array[None], (length, *array.shape)), axi...  95.2 us
    reduce_scatter x1, waiting for transfers between devices, sum_by_chip_2(): pieces = lax.psum_scatter(pieces, core, scatter_dimension=0, tiled=True)  43.9 us
    dot_general x1, matrix products, shards(): preact = jnp.dot(feats, whole_weight, preferred_element_type=jnp.float32)  42.3 us
    dot_general x1, matrix products, shards(): lax.dot_general(feats, local_grad, (((0,), (0,)), ((), ())), preferred_el...  15.9 us
  transfers between devices with their start and end apart: 6, of which 4 were waited for; matrix products, arithmetic and copies ran while one was open for 6% of the time, Pallas kernels for 0%

profile of v1, /device:TPU:0, one launch (start us, length us, event | category | flops | bytes accessed | tf_op | source)
XLA Modules:
  0.0 751.1 jit_solution(17778568095538511045)
XLA Ops:
  7.2 5.8 stack.2
  12.9 0.0 copy-start.1
  12.9 0.0 copy-start.2
  12.9 11.9 %all-to-all-start = ((bf16[64,34,2176]{2,1,0:T(8,128)(2,1)}), bf16[64,34,2176]{2,1,0:T(8,128)(2,1)}, u32[]{:S(2)}, u32[]{:S(2)}) async-start(bf16[64,34,2176]{2,1,0:T(8,128)(2,1)} %stack.2), calls=%async_computation | async-start | bytes 22282240 | tf_op jit(solution)/shard_map/all_to_all | solution.py:60
  24.8 0.0 all-gather.2.cloned.1.call-start
  24.8 0.0 copy-done.1
  24.9 0.0 copy-done.2
  24.9 1.5 pad_maximum_fusion
  26.4 0.0 all-gather.2.cloned.1.call-update
  26.4 0.0 reduce-scatter.3.cloned.1.call-start
  26.5 174.0 %all-gather.2.cloned.1.call-done = bf16[2,2,256,2176]{3,2,1,0:T(8,128)(2,1)} async-done(((bf16[2,1,256,2176]{3,2,1,0:T(8,128)(2,1)}), bf16[2,2,256,2176]{3,2,1,0:T(8,128)(2,1)}) %all-gather.2.cloned.1.call-update) | async-done | bytes 4456464 | tf_op jit(solution)/shard_map/all_gather | solution.py:18
  200.5 6.5 copy.17
  207.0 7.3 dot_general.15
  214.2 0.0 copy-start.3
  214.2 0.0 all-to-all-done
  214.2 13.7 %reshape.39 = bf16[2176,2176]{1,0:T(8,128)(2,1)} reshape(bf16[64,34,2176]{2,1,0:T(8,128)(2,1)} %all-to-all-done) | data formatting | bytes 18939904 | tf_op jit(solution)/shard_map/reshape | solution.py:59
  228.0 0.0 copy-done.3
  228.0 42.3 %convert_reduce_fusion = (f32[2176]{0:T(1024)S(1)}, bf16[1024,2176]{1,0:T(8,128)(2,1)}, f32[1024,2176]{1,0:T(8,128)}, f32[1024,2176]{1,0:T(8,128)}) fusion(bf16[2,512,2176]{2,1,0:T(8,128)(2,1)} %param.9, f32[2176]{0:T(1024)S(1)} %copy-done.3, bf16[1024,2176]{1,0:T(8,128)(2,1)} %bitcast.29, bf16[2176,2176]{1,0:T(8,128)(2,1)} %reshape.39), kind=kOutput, calls=%fused_computation.12 | convolution fusion | flops 9866573824 | bytes 40682496 | tf_op jit(solution)/shard_map/dot_general | solution.py:62
  270.3 15.9 %convolution_bitcast_fusion = f32[2,32,34,2176]{3,2,0,1:T(8,128)S(1)} fusion(bf16[32,2,34,1024]{3,2,1,0:T(8,128)(2,1)} %dot_general.15, bf16[1024,2176]{1,0:T(8,128)(2,1)} %get-tuple-element.6), kind=kOutput, calls=%fused_computation.1 | convolution fusion | flops 9697230848 | bytes 27852800 | tf_op jit(solution)/shard_map/dot_general | solution.py:69
  286.2 12.0 %copy.18 = f32[2,32,34,2176]{3,1,0,2:T(8,128)} copy(f32[2,32,34,2176]{3,2,0,1:T(8,128)S(1)} %convolution_bitcast_fusion) | data formatting | bytes 37879808 | tf_op jit(solution)/shard_map/transpose | solution.py:30
  298.2 0.0 reduce-scatter.3.cloned.1.call-update
  298.2 0.0 all-reduce.3.cloned.1.call-start
  298.2 43.9 %reduce-scatter.3.cloned.1.call-done = f32[32,34,2176]{2,0,1:T(8,128)} async-done(((f32[64,34,2176]{2,0,1:T(8,128)}), f32[32,34,2176]{2,0,1:T(8,128)}) %reduce-scatter.3.cloned.1.call-update) | async-done | bytes 9469968 | tf_op jit(solution)/shard_map/reduce_scatter | solution.py:31
  342.1 0.0 all-reduce.3.cloned.1.call-update
  342.1 0.0 copy-start.4
  342.2 14.9 %convolution_convert_fusion = bf16[1024,2176]{1,0:T(8,128)(2,1)S(1)} fusion(bf16[1024,2176]{1,0:T(8,128)(2,1)} %get-tuple-element.6, bf16[2176,2176]{1,0:T(8,128)(2,1)} %reshape.39), kind=kOutput, calls=%fused_computation.27 | convolution fusion | flops 9699459072 | bytes 18382848 | tf_op jit(solution)/shard_map/dot_general | solution.py:77
  357.1 0.0 copy-start
  357.1 2.1 copy-done
  359.2 0.2 constant_dynamic-slice_fusion.1
  359.4 1.7 collective-permute-start
  361.1 0.0 copy-done.4
  361.1 0.6 dynamic-slice
  361.6 1.1 broadcast_in_dim.2
  362.7 10.0 %all-to-all-start.1 = ((f32[64,1,2176]{2,1,0:T(1,128)}), f32[64,1,2176]{2,1,0:T(1,128)S(1)}, u32[]{:S(2)}, u32[]{:S(2)}) async-start(f32[64,1,2176]{2,1,0:T(1,128)} %broadcast_in_dim.2), calls=%async_computation.2 | async-start | bytes 1114112 | tf_op jit(solution)/shard_map/all_to_all | solution.py:37
  372.7 9.2 %multiply_convert_fusion = bf16[1024,2176]{1,0:T(8,128)(2,1)} fusion(f32[1024,2176]{1,0:T(8,128)} %get-tuple-element.7, f32[1024,2176]{1,0:T(8,128)} %get-tuple-element.8, f32[2176]{0:T(1024)S(1)} %copy-done.3), kind=kLoop, calls=%fused_computation.13 | loop fusion | flops 8912896 | bytes 22290944 | tf_op jit(solution)/shard_map/convert_element_type | solution.py:65
  382.0 95.2 %all-to-all-done.1 = f32[64,1,2176]{2,1,0:T(1,128)S(1)} async-done(((f32[64,1,2176]{2,1,0:T(1,128)}), f32[64,1,2176]{2,1,0:T(1,128)S(1)}, u32[]{:S(2)}, u32[]{:S(2)}) %all-to-all-start.1) | async-done | bytes 557088 | tf_op jit(solution)/shard_map/all_to_all | solution.py:37
  477.2 1.0 reduce_sum.19
  478.2 0.0 collective-permute-done
  478.2 2.8 add_convert_fusion
  481.1 1.1 slice.10
  482.2 1.1 slice.9
  483.3 258.0 %all-reduce.3.cloned.1.call-done = f32[32,34,2176]{2,0,1:T(8,128)} async-done(((f32[32,34,2176]{2,0,1:T(8,128)}), f32[32,34,2176]{2,0,1:T(8,128)}) %all-reduce.3.cloned.1.call-update) | async-done | bytes 9469968
  741.3 2.5 constant_dynamic-slice_fusion
  743.8 0.8 copy.26
Async XLA Ops:
  12.9 11.9 %copy-start.1 = (bf16[2,1,256,1152]{3,2,1,0:T(8,128)(2,1)S(1)}, bf16[2,1,256,1152]{3,2,1,0:T(8,128)(2,1)}, u32[]{:S(2)}) copy-start(bf16[2,1,256,1152]{3,2,1,0:T(8,128)(2,1)} %param.6) | copy-start | bytes 3538948
  12.9 11.9 %copy-start.2 = (bf16[2,1,256,1024]{3,2,1,0:T(8,128)(2,1)S(1)}, bf16[2,1,256,1024]{3,2,1,0:T(8,128)(2,1)}, u32[]{:S(2)}) copy-start(bf16[2,1,256,1024]{3,2,1,0:T(8,128)(2,1)} %param.5) | copy-start | bytes 3145732
  12.9 201.3 %all-to-all-start = ((bf16[64,34,2176]{2,1,0:T(8,128)(2,1)}), bf16[64,34,2176]{2,1,0:T(8,128)(2,1)}, u32[]{:S(2)}, u32[]{:S(2)}) async-start(bf16[64,34,2176]{2,1,0:T(8,128)(2,1)} %stack.2), calls=%async_computation | async-start | bytes 22282240 | tf_op jit(solution)/shard_map/all_to_all | solution.py:60
  24.8 175.7 %all-gather.2.cloned.1.call-start = ((), (), s32[]{:S(2)}) async-start(), calls=%async_computation.3 | async-start | bytes 6684672 | tf_op jit(solution)/shard_map/all_gather | solution.py:18
  26.4 315.7 %reduce-scatter.3.cloned.1.call-start = ((), (), s32[]{:S(2)}) async-start(), calls=%async_computation.4 | async-start | bytes 28409856 | tf_op jit(solution)/shard_map/reduce_scatter | solution.py:31
  214.2 13.7 %copy-start.3 = (f32[2176]{0:T(1024)S(1)}, f32[2176]{0:T(1024)}, u32[]{:S(2)}) copy-start(f32[2176]{0:T(1024)} %param.8) | copy-start | bytes 26116
  298.2 443.1 %all-reduce.3.cloned.1.call-start = ((), (), s32[]{:S(2)}) async-start(), calls=%async_computation.5 | async-start | bytes 18939904
  342.1 18.9 %copy-start.4 = (u32[128]{0:T(128)S(1)}, u32[128]{0:T(128)}, u32[]{:S(2)}) copy-start(u32[128]{0:T(128)} %constant.83) | copy-start | bytes 1540
  357.1 2.2 copy-start
  359.4 118.8 %collective-permute-start = (bf16[2,1,256,2176]{3,2,1,0:T(8,128)(2,1)S(1)}, bf16[2,1,256,2176]{3,2,1,0:T(8,128)(2,1)}, u32[]{:S(2)}, u32[]{:S(2)}) collective-permute-start(bf16[2,1,256,2176]{3,2,1,0:T(8,128)(2,1)S(1)} %constant_dynamic-slice_fusion.1), channel_id=1, source_target_pairs={{0,64},{64,0},{1,65},{65,1},{2,66},{66,2},{3,67},{67,3},{4,68},{68... | collective-permute-start | bytes 6684680 | tf_op jit(solution)/shard_map/ppermute | solution.py:47
  362.7 114.5 %all-to-all-start.1 = ((f32[64,1,2176]{2,1,0:T(1,128)}), f32[64,1,2176]{2,1,0:T(1,128)S(1)}, u32[]{:S(2)}, u32[]{:S(2)}) async-start(f32[64,1,2176]{2,1,0:T(1,128)} %broadcast_in_dim.2), calls=%async_computation.2 | async-start | bytes 1114112 | tf_op jit(solution)/shard_map/all_to_all | solution.py:37
Sparse Core Ops, SparseCore 0:
  27.9 172.5 all-gather.1
  298.3 43.7 reduce-scatter.2
  344.7 396.5 all-reduce.2
